TPU v7x, 256 devices: a whole 4x4x8 slice. The times are simulated.
256 devices in a mesh: rows: 4 (over x), chan: 8 (over y, z_lo), filt: 8 (over z_hi, core).
Axes of the slice: x: 4, y: 4, z: 8 (z_hi: 4, z_lo: 2; z = z_hi * 2 + z_lo), core: 2. Of those that a mesh axis runs over, the one named last changes fastest.
Arguments:
- images: bfloat16 [16, 2048, 2048], P('rows', 'chan', 'filt'), may hold values from -6 to 6
- first_weight: bfloat16 [2048, 1024], P('chan', 'filt'), may hold values from -0.125 to 0.125
- group_weight: bfloat16 [3, 3, 32, 1024], P(None, None, None, 'filt'), may hold values from -0.375 to 0.375
- third_weight: bfloat16 [1024, 2048], P('chan', 'filt'), may hold values from -0.1875 to 0.1875
- out_grad: bfloat16 [16, 2048, 2048], P('rows', 'chan', 'filt'), may hold values from -6 to 6
Outputs:
- block_out: bfloat16 [16, 2048, 2048], P('rows', 'chan', 'filt')
- images_grad: float32 [16, 2048, 2048], P('rows', 'chan', 'filt')
- first_grad: float32 [2048, 1024], P('chan', 'filt')
- group_grad: float32 [3, 3, 32, 1024], P(None, None, None, 'filt')
- third_grad: float32 [1024, 2048], P('chan', 'filt')
All inputs are finite; a program needn't handle non-finite values.
Results may differ from a plain program's by a relative error of at most 0.006.
Values may be sent and summed in bfloat16 or wider, within the bound.
No kernel may reach another device: no remote copies, remote signals or barrier semaphores. Data moves between devices by JAX's collectives and lax.ppermute only.
A program may use at most 128 MiB of HBM per device.

v0:
```python
import jax
import jax.numpy as jnp
from jax import lax
from jax.sharding import PartitionSpec as P


def extended(block, sides, width):
    for axis, dim in sides:
        count = lax.axis_size(axis)
        forward = [(i, i + 1) for i in range(count - 1)]
        backward = [(target, source) for source, target in forward]
        low = lax.ppermute(
            lax.slice_in_dim(block, block.shape[dim] - width, None, axis=dim), axis, forward
        )
        high = lax.ppermute(lax.slice_in_dim(block, 0, width, axis=dim), axis, backward)
        block = jnp.concatenate([low, block, high], axis=dim)
    return block


def silu_slope(values):
    logistic = jax.nn.sigmoid(values)
    return logistic * (1.0 + values * (1.0 - logistic))


def group_conv(padded, kernel, groups_here):
    result = lax.conv_general_dilated(
        padded[None],
        kernel,
        (1, 1),
        "VALID",
        dimension_numbers=("NHWC", "HWIO", "NHWC"),
        feature_group_count=groups_here,
        preferred_element_type=jnp.float32,
    )
    return result[0]


def transposed_kernel(kernel, group_size, groups_here):
    pieces = kernel.reshape(3, 3, group_size, groups_here, group_size)
    swapped = jnp.transpose(pieces, (0, 1, 4, 3, 2)).reshape(
        3, 3, group_size, groups_here * group_size
    )
    return swapped[::-1, ::-1]


def kernel_partial(padded_first, group_delta, group_size, groups_here):
    rows_here = group_delta.shape[0]
    cols_here = group_delta.shape[1]
    pixels = rows_here * cols_here
    delta_groups = group_delta.reshape(pixels, groups_here, group_size)
    kernel_terms = []
    for row_shift in range(3):
        for col_shift in range(3):
            window = padded_first[
                row_shift : row_shift + rows_here, col_shift : col_shift + cols_here
            ]
            window = window.reshape(pixels, groups_here, group_size)
            kernel_terms.append(
                jnp.einsum("pgi,pgo->gio", window, delta_groups, preferred_element_type=jnp.float32)
            )
    kernel_part = jnp.stack(kernel_terms).reshape(3, 3, groups_here, group_size, group_size)
    kernel_part = jnp.transpose(kernel_part, (0, 1, 3, 2, 4))
    return kernel_part.reshape(3, 3, group_size, groups_here * group_size)


def body(images, first_weight, group_weight, third_weight, out_grad):
    rows_here = images.shape[0]
    cols_here = images.shape[1]
    group_size = group_weight.shape[2]
    first_panel, third_panel = (
        lax.all_gather(first_weight, "chan", axis=0, tiled=True),
        lax.all_gather(third_weight, "chan", axis=0, tiled=True),
    )
    pixels = rows_here * cols_here
    groups_here = group_weight.shape[3] // group_size
    gathered = lax.all_gather(images, "filt", axis=2, tiled=True)
    flat_images = gathered.reshape(pixels, gathered.shape[2])
    pre_first = jnp.dot(flat_images, first_panel, preferred_element_type=jnp.float32)
    act_first = (
        jax.nn.silu(pre_first)
        .astype(jnp.bfloat16)
        .reshape(rows_here, cols_here, first_panel.shape[1])
    )
    padded_first = extended(act_first, (("rows", 0), ("chan", 1)), 1)
    pre_group = group_conv(padded_first, group_weight, groups_here)
    act_group = jax.nn.silu(pre_group).astype(jnp.bfloat16)
    mid_whole = lax.all_gather(act_group, "filt", axis=2, tiled=True)
    flat_mid = mid_whole.reshape(pixels, mid_whole.shape[2])
    third_out = jnp.dot(flat_mid, third_panel, preferred_element_type=jnp.float32)
    own_images = images.reshape(pixels, images.shape[2]).astype(jnp.float32)
    block_out = (own_images + third_out).astype(jnp.bfloat16).reshape(images.shape)
    grad_flat = out_grad.reshape(pixels, out_grad.shape[2])
    mid_terms = lax.dot_general(
        grad_flat, third_panel, (((1,), (1,)), ((), ())), preferred_element_type=jnp.float32
    )
    mid_grad = lax.psum_scatter(
        mid_terms.reshape(rows_here, cols_here, mid_terms.shape[1]),
        "filt",
        scatter_dimension=2,
        tiled=True,
    )
    third_part = lax.dot_general(
        flat_mid, grad_flat, (((0,), (0,)), ((), ())), preferred_element_type=jnp.float32
    )
    group_delta = (mid_grad * silu_slope(pre_group)).astype(jnp.bfloat16)
    padded_delta = extended(group_delta, (("rows", 0), ("chan", 1)), 1)
    first_back = group_conv(
        padded_delta, transposed_kernel(group_weight, group_size, groups_here), groups_here
    )
    kernel_part = kernel_partial(padded_first, group_delta, group_size, groups_here)
    first_delta = (first_back.reshape(pixels, first_back.shape[2]) * silu_slope(pre_first)).astype(
        jnp.bfloat16
    )
    first_part = lax.dot_general(
        flat_images, first_delta, (((0,), (0,)), ((), ())), preferred_element_type=jnp.float32
    )
    input_terms = lax.dot_general(
        first_delta, first_panel, (((1,), (1,)), ((), ())), preferred_element_type=jnp.float32
    )
    back_images = lax.psum_scatter(
        input_terms.reshape(rows_here, cols_here, input_terms.shape[1]).astype(jnp.bfloat16),
        "filt",
        scatter_dimension=2,
        tiled=True,
    ).astype(jnp.float32)
    images_grad = out_grad.astype(jnp.float32) + back_images
    group_grad = lax.psum(kernel_part, ("rows", "chan"))
    first_total, third_total = lax.psum((first_part, third_part), "rows")
    first_grad, third_grad = (
        lax.psum_scatter(first_total, "chan", scatter_dimension=0, tiled=True),
        lax.psum_scatter(third_total, "chan", scatter_dimension=0, tiled=True),
    )
    return (block_out, images_grad, first_grad, group_grad, third_grad)


def solution(mesh):
    in_specs = (
        P("rows", "chan", "filt"),
        P("chan", "filt"),
        P(None, None, None, "filt"),
        P("chan", "filt"),
        P("rows", "chan", "filt"),
    )
    out_specs = (
        P("rows", "chan", "filt"),
        P("rows", "chan", "filt"),
        P("chan", "filt"),
        P(None, None, None, "filt"),
        P("chan", "filt"),
    )
    return jax.shard_map(body, mesh=mesh, in_specs=in_specs, out_specs=out_specs, check_vma=False)
```

profile of v0, /device:TPU:32, one launch (start us, length us, event | category | flops | bytes accessed | tf_op | source)
XLA Modules:
  0.0 700.0 jit_solution(2654013649618200023)
XLA Ops:
  7.9 39.6 %all_gather.15 = bf16[1024,256]{1,0:T(8,128)(2,1)S(1)} all-gather(bf16[128,256]{1,0:T(8,128)(2,1)} %param.8), channel_id=1, replica_groups=mesh['rows'=4,'chan'=8,'filt'=8] {'chan'}, dimensions={0}, use_global_device_ids=true | all-gather | bytes 589824 | tf_op jit(solution)/shard_map/all_gather | solution.py:72
  47.5 3.8 fusion.10
  52.2 36.9 %all_gather.13 = bf16[2048,128]{1,0:T(8,128)(2,1)S(1)} all-gather(bf16[256,128]{1,0:T(8,128)(2,1)S(1)} %copy-done.13), channel_id=1, replica_groups=mesh['rows'=4,'chan'=8,'filt'=8] {'chan'}, dimensions={0}, use_global_device_ids=true | all-gather | bytes 589824 | tf_op jit(solution)/shard_map/all_gather | solution.py:71
  89.1 4.4 multiply_convert_fusion.3
  93.5 2.9 collective-permute-start
  98.4 4.2 collective-permute-done.1
  103.2 3.4 collective-permute-start.2
  106.6 3.2 collective-permute-start.3
  110.7 8.0 %collective-permute-done.2 = bf16[6,1,128]{1,2,0:T(8,128)(2,1)S(1)} collective-permute-done((bf16[6,1,128]{1,2,0:T(8,128)(2,1)S(1)}, bf16[6,1,128]{1,2,0:T(8,128)(2,1)S(1)}, u32[]{:S(2)}, u32[]{:S(2)}) %collective-permute-start.2) | collective-permute-done | bytes 1568 | tf_op jit(solution)/shard_map/ppermute | solution.py:12
  118.7 10.6 %collective-permute-done.3 = bf16[6,1,128]{1,2,0:T(8,128)(2,1)S(1)} collective-permute-done((bf16[6,1,128]{1,2,0:T(8,128)(2,1)S(1)}, bf16[6,1,128]{1,2,0:T(8,128)(2,1)S(1)}, u32[]{:S(2)}, u32[]{:S(2)}) %collective-permute-start.3) | collective-permute-done | bytes 1568 | tf_op jit(solution)/shard_map/ppermute | solution.py:15
  130.0 5.8 copy.36
  135.8 9.4 %fusion.13 = f32[1,4,256,4,32]{4,0,3,2,1:T(1,128)S(1)} fusion(bf16[1,6,258,4,32]{4,0,3,2,1:T(2,128)(2,1)} %copy.36, bf16[3,3,32,4,32]{4,3,2,1,0:T(4,128)(2,1)} %shard_map.94), kind=kOutput, calls=%fused_computation.39 | convolution fusion | flops 75497472 | bytes 994304 | tf_op jit(solution)/shard_map/conv_general_dilated | solution.py:26
  145.3 3.5 copy.38
  150.2 2.0 multiply_convert_fusion.1
  152.2 3.3 collective-permute-start.4
  157.5 4.3 collective-permute-done.5
  161.8 3.5 collective-permute-start.6
  165.3 2.6 collective-permute-start.7
  169.2 2.5 collective-permute-done.7
  172.1 5.9 copy.44
  178.0 13.8 %convolution_reduce_fusion = f32[4,256,4,32]{3,2,1,0:T(4,128)S(1)} fusion(bf16[1,6,258,4,32]{4,0,3,2,1:T(2,128)(2,1)} %copy.44, bf16[3,3,32,4,32]{4,3,2,1,0:T(4,128)(2,1)} %rev.6), kind=kOutput, calls=%fused_computation.2 | convolution fusion | flops 75497472 | bytes 994304 | tf_op jit(solution)/shard_map/conv_general_dilated | solution.py:26
  194.9 4.0 convolution_bitcast_fusion
  199.0 3.4 convolution_bitcast_fusion.1
  202.4 40.0 %reduce-scatter.9.cloned.1.call-done = f32[256,128]{0,1:T(8,128)} async-done(((f32[2048,128]{0,1:T(8,128)}), f32[256,128]{0,1:T(8,128)}) %reduce-scatter.9.cloned.1.call-update) | async-done | bytes 131088 | tf_op jit(solution)/shard_map/reduce_scatter | solution.py:130
  242.4 44.5 %reduce-scatter.11.cloned.1.call-done = f32[128,256]{1,0:T(8,128)} async-done(((f32[1024,256]{1,0:T(8,128)}), f32[128,256]{1,0:T(8,128)}) %reduce-scatter.11.cloned.1.call-update) | async-done | bytes 131088 | tf_op jit(solution)/shard_map/reduce_scatter | solution.py:131
  286.9 3.2 convolution_convert_fusion
  294.3 1.8 reshape.85
  312.5 3.2 fusion
  315.6 21.3 %all-reduce.6.cloned.1.call-done = (f32[256,128]{0,1:T(8,128)}, f32[128,256]{1,0:T(8,128)}) async-done(((f32[256,128]{0,1:T(8,128)}, f32[128,256]{1,0:T(8,128)}), (f32[256,128]{0,1:T(8,128)}, f32[128,256]{1,0:T(8,128)})) %all-reduce.6.cloned.1.call-update) | async-done | bytes 262160 | tf_op jit(solution)/shard_map/psum | solution.py:128
  338.7 59.3 %reduce-scatter.7.cloned.1.call-done = bf16[4,256,256]{2,1,0:T(8,128)(2,1)} async-done(((bf16[4,256,2048]{2,1,0:T(8,128)(2,1)}), bf16[4,256,256]{2,1,0:T(8,128)(2,1)}) %reduce-scatter.7.cloned.1.call-update) | async-done | bytes 524304 | tf_op jit(solution)/shard_map/reduce_scatter | solution.py:120
  398.0 2.1 convert_add_fusion
  400.1 290.7 %all-reduce.4.cloned.1.call-done = f32[3,3,32,128]{3,2,1,0:T(8,128)} async-done(((f32[3,3,32,128]{3,2,1,0:T(8,128)}), f32[3,3,32,128]{3,2,1,0:T(8,128)}) %all-reduce.4.cloned.1.call-update) | async-done | bytes 147472 | tf_op jit(solution)/shard_map/psum | solution.py:127
  (106 shorter events, 38.3 us)
Async XLA Ops:
  7.2 81.9 %all-gather.3.cloned.1.call-start = ((), (), s32[]{:S(2)}) async-start(), calls=%async_computation.4 | async-start | bytes 4718592 | tf_op jit(solution)/shard_map/all_gather | solution.py:76
  7.9 142.2 %reduce-scatter.5.cloned.1.call-start = ((), (), s32[]{:S(2)}) async-start(), calls=%async_computation.6 | async-start | bytes 4718592 | tf_op jit(solution)/shard_map/reduce_scatter | solution.py:96
  51.3 0.8 copy-start.13
  51.4 147.6 %all-gather.5.cloned.1.call-start = ((), (), s32[]{:S(2)}) async-start(), calls=%async_computation.5 | async-start | bytes 2359296 | tf_op jit(solution)/shard_map/all_gather | solution.py:87
  89.1 4.4 copy-start
  93.5 16.3 %copy-start.12 = (bf16[3,3,32,128]{3,2,1,0:T(8,128)(2,1)S(1)}, bf16[3,3,32,128]{3,2,1,0:T(8,128)(2,1)}, u32[]{:S(2)}) copy-start(bf16[3,3,32,128]{3,2,1,0:T(8,128)(2,1)} %param.7) | copy-start | bytes 221188
  93.5 4.8 collective-permute-start
  96.4 6.2 collective-permute-start.1
  98.3 4.6 copy-start.7
  102.6 0.6 copy-start.9
  103.2 15.5 %collective-permute-start.2 = (bf16[6,1,128]{1,2,0:T(8,128)(2,1)S(1)}, bf16[6,1,128]{1,2,0:T(8,128)(2,1)S(1)}, u32[]{:S(2)}, u32[]{:S(2)}) collective-permute-start(bf16[6,1,128]{1,2,0:T(8,128)(2,1)S(1)} %get-tuple-element.29), channel_id=1, source_target_pairs={{0,8},{8,16},{16,24},{24,32},{32,40},{40,48},{48,56},{1,9},{9,17},... | collective-permute-start | bytes 4616 | tf_op jit(solution)/shard_map/ppermute | solution.py:12
  106.6 22.7 %collective-permute-start.3 = (bf16[6,1,128]{1,2,0:T(8,128)(2,1)S(1)}, bf16[6,1,128]{1,2,0:T(8,128)(2,1)S(1)}, u32[]{:S(2)}, u32[]{:S(2)}) collective-permute-start(bf16[6,1,128]{1,2,0:T(8,128)(2,1)S(1)} %get-tuple-element.30), channel_id=1, source_target_pairs={{8,0},{16,8},{24,16},{32,24},{40,32},{48,40},{56,48},{9,1},{17,9},... | collective-permute-start | bytes 4616 | tf_op jit(solution)/shard_map/ppermute | solution.py:15
  118.7 17.1 %copy-start.4 = (bf16[6,1,128]{1,2,0:T(8,128)(2,1)}, bf16[6,1,128]{1,2,0:T(8,128)(2,1)S(1)}, u32[]{:S(2)}) copy-start(bf16[6,1,128]{1,2,0:T(8,128)(2,1)S(1)} %collective-permute-done.2) | copy-start | bytes 4612
  129.3 0.7 copy-start.6
  148.8 19.0 %copy-start.3 = (bf16[3,3,32,4,32]{4,3,2,1,0:T(4,128)(2,1)S(1)}, bf16[3,3,32,4,32]{4,3,2,1,0:T(4,128)(2,1)}, u32[]{:S(2)}) copy-start(bf16[3,3,32,4,32]{4,3,2,1,0:T(4,128)(2,1)} %shard_map.94) | copy-start | bytes 221188
  152.2 90.2 %reduce-scatter.9.cloned.1.call-start = ((), (), s32[]{:S(2)}) async-start(), calls=%async_computation.9 | async-start | bytes 1179648 | tf_op jit(solution)/shard_map/reduce_scatter | solution.py:130
  152.2 5.2 collective-permute-start.4
  155.6 6.2 collective-permute-start.5
  161.8 7.4 %collective-permute-start.6 = (bf16[6,1,128]{2,1,0:T(2,128)(2,1)S(1)}, bf16[6,1,128]{2,1,0:T(2,128)(2,1)S(1)}, u32[]{:S(2)}, u32[]{:S(2)}) collective-permute-start(bf16[6,1,128]{2,1,0:T(2,128)(2,1)S(1)} %get-tuple-element.27), channel_id=1, source_target_pairs={{0,8},{8,16},{16,24},{24,32},{32,40},{40,48},{48,56},{1,9},{9,17},... | collective-permute-start | bytes 4616 | tf_op jit(solution)/shard_map/ppermute | solution.py:12
  165.3 6.4 collective-permute-start.7
  194.9 4.1 copy-start.2
  198.9 88.0 %copy-start.1 = (bf16[2048,128]{1,0:T(8,128)(2,1)S(1)}, bf16[2048,128]{1,0:T(8,128)(2,1)}, u32[]{:S(2)}) copy-start(bf16[2048,128]{1,0:T(8,128)(2,1)} %copy-done) | copy-start | bytes 1572868
  198.9 88.0 %reduce-scatter.11.cloned.1.call-start = ((), (), s32[]{:S(2)}) async-start(), calls=%async_computation.10 | async-start | bytes 1179648 | tf_op jit(solution)/shard_map/reduce_scatter | solution.py:131
  202.4 134.6 %all-reduce.6.cloned.1.call-start = ((), (), s32[]{:S(2)}) async-start(), calls=%async_computation.11 | async-start | bytes 524288 | tf_op jit(solution)/shard_map/psum | solution.py:128
  286.9 111.1 %reduce-scatter.7.cloned.1.call-start = ((), (), s32[]{:S(2)}) async-start(), calls=%async_computation.7 | async-start | bytes 4718592 | tf_op jit(solution)/shard_map/reduce_scatter | solution.py:120
  290.2 0.8 copy-start.8
  290.2 0.9 copy-start.10
  290.2 1.6 copy-start.5
  290.2 400.7 %all-reduce.4.cloned.1.call-start = ((), (), s32[]{:S(2)}) async-start(), calls=%async_computation.8 | async-start | bytes 294912 | tf_op jit(solution)/shard_map/psum | solution.py:127
  337.0 355.5 %copy-start.11 = (f32[128,256]{1,0:T(8,128)S(1)}, f32[128,256]{1,0:T(8,128)}, u32[]{:S(2)}) copy-start(f32[128,256]{1,0:T(8,128)} %get-tuple-element.46) | copy-start | bytes 393220
Sparse Core Ops, SparseCore 0:
  9.8 60.3 all-gather.2
  72.7 76.7 reduce-scatter.4
  152.3 42.8 all-gather.4
  199.0 43.3 reduce-scatter.8
  244.8 42.0 reduce-scatter.10
  289.1 47.8 all-reduce.5
  339.7 58.2 reduce-scatter.6
  401.4 289.4 all-reduce.3
where the time goes:
time: 701 us; the launch traced here: 700 us
  waiting for transfers between devices  487 us (69%)
  blocking collectives  76.5 us (11%)
  matrix products  49 us (7%)
  local copies, waits for them, and re-layouts  43.4 us (6%)
  starting transfers between devices  22 us (3%)
  between operations  14.5 us (2%)
  other arithmetic  7.29 us (1%)
    psum x1, waiting for transfers between devices, body(): group_grad = lax.psum(kernel_part, ('rows', 'chan'))  291 us
    reduce_scatter x1, waiting for transfers between devices, body(): lax.psum_scatter(input_terms.reshape(rows_here, cols_here, input_terms.sh...  59.3 us
    reduce_scatter x1, waiting for transfers between devices, body(): lax.psum_scatter(third_total, 'chan', scatter_dimension=0, tiled=True)  44.5 us
    reduce_scatter x1, waiting for transfers between devices, body(): lax.psum_scatter(first_total, 'chan', scatter_dimension=0, tiled=True)  40 us
    all_gather x1, blocking collectives, body(): lax.all_gather(third_weight, 'chan', axis=0, tiled=True)  39.6 us
    all_gather x1, blocking collectives, body(): lax.all_gather(first_weight, 'chan', axis=0, tiled=True)  36.9 us
    conv_general_dilated x2, matrix products, group_conv(): lax.conv_general_dilated(padded[None], kernel, (1, 1), 'VALID', dimension...  23.3 us
    ppermute x4, waiting for transfers between devices, extended(): lax.ppermute(lax.slice_in_dim(block, 0, width, axis=dim), axis, backward)  21.5 us
  transfers between devices with their start and end apart: 16, of which 12 were waited for; matrix products, arithmetic and copies ran while one was open for 13% of the time, Pallas kernels for 0%

commit v1 on v0

--- a/solution.py
+++ b/solution.py
@@ -124,7 +124,8 @@
         tiled=True,
     ).astype(jnp.float32)
     images_grad = out_grad.astype(jnp.float32) + back_images
-    group_grad = lax.psum(kernel_part, ("rows", "chan"))
+    parts = lax.all_gather(kernel_part, ("rows", "chan"), axis=0, tiled=False)
+    group_grad = parts.sum(axis=0)
     first_total, third_total = lax.psum((first_part, third_part), "rows")
     first_grad, third_grad = (
         lax.psum_scatter(first_total, "chan", scatter_dimension=0, tiled=True),

time: 701 us -> 586 us (0.84)
  waiting for transfers between devices: 487 us -> 375 us
    psum x1 -> x0, waiting for transfers between devices: 291 us -> none  [body(): group_grad = lax.psum(kernel_part, ('rows', 'chan'))]
    all_gather x0 -> x1, waiting for transfers between devices: none -> 174 us  [body(): parts = lax.all_gather(kernel_part, ('rows', 'chan'), axis=0, tiled=False)]
  transfers between devices with their start and end apart: 16 -> 16, of which waited for: 12 -> 12; matrix products, arithmetic and copies ran while one was open for 13% -> 15% of each run, Pallas kernels for 0% -> 0%
where the time goes in v1:
time: 586 us; the launch traced here: 585 us
  waiting for transfers between devices  375 us (64%)
  blocking collectives  76.5 us (13%)
  matrix products  49 us (8%)
  local copies, waits for them, and re-layouts  39.2 us (7%)
  starting transfers between devices  20.8 us (4%)
  between operations  14.5 us (2%)
  other arithmetic  9.81 us (2%)
    all_gather x1, waiting for transfers between devices, body(): parts = lax.all_gather(kernel_part, ('rows', 'chan'), axis=0, tiled=False)  174 us
    reduce_scatter x1, waiting for transfers between devices, body(): lax.psum_scatter(input_terms.reshape(rows_here, cols_here, input_terms.sh...  59.4 us
    reduce_scatter x1, waiting for transfers between devices, body(): lax.psum_scatter(third_total, 'chan', scatter_dimension=0, tiled=True)  44.3 us
    reduce_scatter x1, waiting for transfers between devices, body(): lax.psum_scatter(first_total, 'chan', scatter_dimension=0, tiled=True)  40 us
    all_gather x1, blocking collectives, body(): lax.all_gather(third_weight, 'chan', axis=0, tiled=True)  39.6 us
    all_gather x1, blocking collectives, body(): lax.all_gather(first_weight, 'chan', axis=0, tiled=True)  36.9 us
    psum x1, waiting for transfers between devices, body(): first_total, third_total = lax.psum((first_part, third_part), 'rows')  24.9 us
    conv_general_dilated x2, matrix products, group_conv(): lax.conv_general_dilated(padded[None], kernel, (1, 1), 'VALID', dimension...  23.3 us
  transfers between devices with their start and end apart: 16, of which 12 were waited for; matrix products, arithmetic and copies ran while one was open for 15% of the time, Pallas kernels for 0%

profile of v1, /device:TPU:32, one launch (start us, length us, event | category | flops | bytes accessed | tf_op | source)
XLA Modules:
  0.0 584.7 jit_solution(12277533981861192721)
XLA Ops:
  7.9 39.6 %all_gather.18 = bf16[1024,256]{1,0:T(8,128)(2,1)S(1)} all-gather(bf16[128,256]{1,0:T(8,128)(2,1)} %param.8), channel_id=1, replica_groups=mesh['rows'=4,'chan'=8,'filt'=8] {'chan'}, dimensions={0}, use_global_device_ids=true | all-gather | bytes 589824 | tf_op jit(solution)/shard_map/all_gather | solution.py:72
  47.5 3.8 fusion.10
  52.2 36.9 %all_gather.16 = bf16[2048,128]{1,0:T(8,128)(2,1)S(1)} all-gather(bf16[256,128]{1,0:T(8,128)(2,1)S(1)} %copy-done.16), channel_id=1, replica_groups=mesh['rows'=4,'chan'=8,'filt'=8] {'chan'}, dimensions={0}, use_global_device_ids=true | all-gather | bytes 589824 | tf_op jit(solution)/shard_map/all_gather | solution.py:71
  89.1 4.4 multiply_convert_fusion.3
  93.5 2.9 collective-permute-start
  98.4 4.2 collective-permute-done.1
  103.2 3.4 collective-permute-start.2
  106.6 3.2 collective-permute-start.3
  110.7 8.0 %collective-permute-done.2 = bf16[6,1,128]{1,2,0:T(8,128)(2,1)S(1)} collective-permute-done((bf16[6,1,128]{1,2,0:T(8,128)(2,1)S(1)}, bf16[6,1,128]{1,2,0:T(8,128)(2,1)S(1)}, u32[]{:S(2)}, u32[]{:S(2)}) %collective-permute-start.2) | collective-permute-done | bytes 1568 | tf_op jit(solution)/shard_map/ppermute | solution.py:12
  118.7 11.4 %collective-permute-done.3 = bf16[6,1,128]{1,2,0:T(8,128)(2,1)S(1)} collective-permute-done((bf16[6,1,128]{1,2,0:T(8,128)(2,1)S(1)}, bf16[6,1,128]{1,2,0:T(8,128)(2,1)S(1)}, u32[]{:S(2)}, u32[]{:S(2)}) %collective-permute-start.3) | collective-permute-done | bytes 1568 | tf_op jit(solution)/shard_map/ppermute | solution.py:15
  130.8 5.8 copy.63
  136.6 9.4 %fusion.13 = f32[1,4,256,4,32]{4,0,3,2,1:T(1,128)S(1)} fusion(bf16[1,6,258,4,32]{4,0,3,2,1:T(2,128)(2,1)} %copy.63, bf16[3,3,32,4,32]{4,3,2,1,0:T(4,128)(2,1)} %shard_map.94), kind=kOutput, calls=%fused_computation.40 | convolution fusion | flops 75497472 | bytes 994304 | tf_op jit(solution)/shard_map/conv_general_dilated | solution.py:26
  146.0 3.5 copy.65
  150.9 2.0 multiply_convert_fusion.1
  153.0 2.2 collective-permute-start.4
  157.0 4.3 collective-permute-done.5
  161.3 3.9 collective-permute-start.6
  165.3 2.1 collective-permute-start.7
  168.7 2.9 collective-permute-done.7
  172.1 5.9 %copy.71 = bf16[1,6,258,4,32]{4,0,3,2,1:T(2,128)(2,1)} copy(bf16[1,6,258,4,32]{2,4,3,1,0:T(8,128)(2,1)S(1)} %bitcast.121) | data formatting | bytes 792576 | tf_op jit(solution)/shard_map/broadcast_in_dim | solution.py:27
  177.9 13.8 %convolution_reduce_fusion = f32[4,256,4,32]{3,2,1,0:T(4,128)S(1)} fusion(bf16[1,6,258,4,32]{4,0,3,2,1:T(2,128)(2,1)} %copy.71, bf16[3,3,32,4,32]{4,3,2,1,0:T(4,128)(2,1)} %rev.6), kind=kOutput, calls=%fused_computation.2 | convolution fusion | flops 75497472 | bytes 994304 | tf_op jit(solution)/shard_map/conv_general_dilated | solution.py:26
  194.9 4.0 convolution_bitcast_fusion
  199.0 3.4 convolution_bitcast_fusion.1
  202.4 40.0 %reduce-scatter.9.cloned.1.call-done = f32[256,128]{0,1:T(8,128)} async-done(((f32[2048,128]{0,1:T(8,128)}), f32[256,128]{0,1:T(8,128)}) %reduce-scatter.9.cloned.1.call-update) | async-done | bytes 131088 | tf_op jit(solution)/shard_map/reduce_scatter | solution.py:131
  242.4 44.3 %reduce-scatter.11.cloned.1.call-done = f32[128,256]{1,0:T(8,128)} async-done(((f32[1024,256]{1,0:T(8,128)}), f32[128,256]{1,0:T(8,128)}) %reduce-scatter.11.cloned.1.call-update) | async-done | bytes 131088 | tf_op jit(solution)/shard_map/reduce_scatter | solution.py:132
  286.8 3.3 convolution_convert_fusion
  308.9 3.1 fusion
  312.0 24.9 %all-reduce.3.cloned.1.call-done = (f32[256,128]{0,1:T(8,128)}, f32[128,256]{1,0:T(8,128)}) async-done(((f32[256,128]{0,1:T(8,128)}, f32[128,256]{1,0:T(8,128)}), (f32[256,128]{0,1:T(8,128)}, f32[128,256]{1,0:T(8,128)})) %all-reduce.3.cloned.1.call-update) | async-done | bytes 262160 | tf_op jit(solution)/shard_map/psum | solution.py:129
  338.5 59.4 %reduce-scatter.7.cloned.1.call-done = bf16[4,256,256]{2,1,0:T(8,128)(2,1)} async-done(((bf16[4,256,2048]{2,1,0:T(8,128)(2,1)}), bf16[4,256,256]{2,1,0:T(8,128)(2,1)}) %reduce-scatter.7.cloned.1.call-update) | async-done | bytes 524304 | tf_op jit(solution)/shard_map/reduce_scatter | solution.py:120
  397.9 2.1 convert_add_fusion
  400.0 173.8 %all-gather.8.cloned.1.call-done = f32[32,3,3,32,128]{4,3,2,1,0:T(8,128)} async-done(((f32[1,3,3,32,128]{4,3,2,1,0:T(8,128)}), f32[32,3,3,32,128]{4,3,2,1,0:T(8,128)}) %all-gather.8.cloned.1.call-update) | async-done | bytes 4718608 | tf_op jit(solution)/shard_map/all_gather | solution.py:127
  573.8 3.4 reduce_sum.9
  (112 shorter events, 35.0 us)
Async XLA Ops:
  7.2 81.9 %all-gather.4.cloned.1.call-start = ((), (), s32[]{:S(2)}) async-start(), calls=%async_computation.4 | async-start | bytes 4718592 | tf_op jit(solution)/shard_map/all_gather | solution.py:76
  7.9 143.0 %reduce-scatter.5.cloned.1.call-start = ((), (), s32[]{:S(2)}) async-start(), calls=%async_computation.6 | async-start | bytes 4718592 | tf_op jit(solution)/shard_map/reduce_scatter | solution.py:96
  51.4 0.8 copy-start.16
  51.4 147.6 %all-gather.6.cloned.1.call-start = ((), (), s32[]{:S(2)}) async-start(), calls=%async_computation.5 | async-start | bytes 2359296 | tf_op jit(solution)/shard_map/all_gather | solution.py:87
  89.1 4.4 copy-start
  93.5 16.3 %copy-start.15 = (bf16[3,3,32,128]{3,2,1,0:T(8,128)(2,1)S(1)}, bf16[3,3,32,128]{3,2,1,0:T(8,128)(2,1)}, u32[]{:S(2)}) copy-start(bf16[3,3,32,128]{3,2,1,0:T(8,128)(2,1)} %param.7) | copy-start | bytes 221188
  93.5 4.8 collective-permute-start
  96.4 6.2 %collective-permute-start.1 = (bf16[1,256,128]{2,1,0:T(8,128)(2,1)S(1)}, bf16[1,256,128]{2,1,0:T(8,128)(2,1)S(1)}, u32[]{:S(2)}, u32[]{:S(2)}) collective-permute-start(bf16[1,256,128]{2,1,0:T(8,128)(2,1)S(1)} %get-tuple-element.41), channel_id=1, source_target_pairs={{64,0},{128,64},{192,128},{65,1},{129,65},{193,129},{66,2},{130,66... | collective-permute-start | bytes 196616 | tf_op jit(solution)/shard_map/ppermute | solution.py:15
  98.3 4.6 copy-start.10
  103.2 15.5 %collective-permute-start.2 = (bf16[6,1,128]{1,2,0:T(8,128)(2,1)S(1)}, bf16[6,1,128]{1,2,0:T(8,128)(2,1)S(1)}, u32[]{:S(2)}, u32[]{:S(2)}) collective-permute-start(bf16[6,1,128]{1,2,0:T(8,128)(2,1)S(1)} %get-tuple-element.34), channel_id=1, source_target_pairs={{0,8},{8,16},{16,24},{24,32},{32,40},{40,48},{48,56},{1,9},{9,17},... | collective-permute-start | bytes 4616 | tf_op jit(solution)/shard_map/ppermute | solution.py:12
  106.6 23.5 %collective-permute-start.3 = (bf16[6,1,128]{1,2,0:T(8,128)(2,1)S(1)}, bf16[6,1,128]{1,2,0:T(8,128)(2,1)S(1)}, u32[]{:S(2)}, u32[]{:S(2)}) collective-permute-start(bf16[6,1,128]{1,2,0:T(8,128)(2,1)S(1)} %get-tuple-element.35), channel_id=1, source_target_pairs={{8,0},{16,8},{24,16},{32,24},{40,32},{48,40},{56,48},{9,1},{17,9},... | collective-permute-start | bytes 4616 | tf_op jit(solution)/shard_map/ppermute | solution.py:15
  118.7 17.9 %copy-start.5 = (bf16[6,1,128]{1,2,0:T(8,128)(2,1)}, bf16[6,1,128]{1,2,0:T(8,128)(2,1)S(1)}, u32[]{:S(2)}) copy-start(bf16[6,1,128]{1,2,0:T(8,128)(2,1)S(1)} %collective-permute-done.2) | copy-start | bytes 4612
  130.1 0.7 copy-start.7
  149.6 17.8 %copy-start.3 = (bf16[3,3,32,4,32]{4,3,2,1,0:T(4,128)(2,1)S(1)}, bf16[3,3,32,4,32]{4,3,2,1,0:T(4,128)(2,1)}, u32[]{:S(2)}) copy-start(bf16[3,3,32,4,32]{4,3,2,1,0:T(4,128)(2,1)} %shard_map.94) | copy-start | bytes 221188
  152.9 89.5 %reduce-scatter.9.cloned.1.call-start = ((), (), s32[]{:S(2)}) async-start(), calls=%async_computation.9 | async-start | bytes 1179648 | tf_op jit(solution)/shard_map/reduce_scatter | solution.py:131
  153.0 4.1 collective-permute-start.4
  155.2 6.2 %collective-permute-start.5 = (bf16[1,256,128]{2,1,0:T(8,128)(2,1)S(1)}, bf16[1,256,128]{2,1,0:T(8,128)(2,1)S(1)}, u32[]{:S(2)}, u32[]{:S(2)}) collective-permute-start(bf16[1,256,128]{2,1,0:T(8,128)(2,1)S(1)} %get-tuple-element.39), channel_id=1, source_target_pairs={{64,0},{128,64},{192,128},{65,1},{129,65},{193,129},{66,2},{130,66... | collective-permute-start | bytes 196616 | tf_op jit(solution)/shard_map/ppermute | solution.py:15
  161.3 7.4 %collective-permute-start.6 = (bf16[6,1,128]{2,1,0:T(2,128)(2,1)S(1)}, bf16[6,1,128]{2,1,0:T(2,128)(2,1)S(1)}, u32[]{:S(2)}, u32[]{:S(2)}) collective-permute-start(bf16[6,1,128]{2,1,0:T(2,128)(2,1)S(1)} %get-tuple-element.32), channel_id=1, source_target_pairs={{0,8},{8,16},{16,24},{24,32},{32,40},{40,48},{48,56},{1,9},{9,17},... | collective-permute-start | bytes 4616 | tf_op jit(solution)/shard_map/ppermute | solution.py:12
  165.3 6.4 %collective-permute-start.7 = (bf16[6,1,128]{2,1,0:T(2,128)(2,1)S(1)}, bf16[6,1,128]{2,1,0:T(2,128)(2,1)S(1)}, u32[]{:S(2)}, u32[]{:S(2)}) collective-permute-start(bf16[6,1,128]{2,1,0:T(2,128)(2,1)S(1)} %get-tuple-element.33), channel_id=1, source_target_pairs={{8,0},{16,8},{24,16},{32,24},{40,32},{48,40},{56,48},{9,1},{17,9},... | collective-permute-start | bytes 4616 | tf_op jit(solution)/shard_map/ppermute | solution.py:15
  194.9 4.1 copy-start.2
  198.9 87.9 %copy-start.1 = (bf16[2048,128]{1,0:T(8,128)(2,1)S(1)}, bf16[2048,128]{1,0:T(8,128)(2,1)}, u32[]{:S(2)}) copy-start(bf16[2048,128]{1,0:T(8,128)(2,1)} %copy-done) | copy-start | bytes 1572868
  198.9 87.8 %reduce-scatter.11.cloned.1.call-start = ((), (), s32[]{:S(2)}) async-start(), calls=%async_computation.10 | async-start | bytes 1179648 | tf_op jit(solution)/shard_map/reduce_scatter | solution.py:132
  202.4 134.5 %all-reduce.3.cloned.1.call-start = ((), (), s32[]{:S(2)}) async-start(), calls=%async_computation.11 | async-start | bytes 524288 | tf_op jit(solution)/shard_map/psum | solution.py:129
  286.8 111.2 %reduce-scatter.7.cloned.1.call-start = ((), (), s32[]{:S(2)}) async-start(), calls=%async_computation.7 | async-start | bytes 4718592 | tf_op jit(solution)/shard_map/reduce_scatter | solution.py:120
  290.1 0.8 copy-start.11
  290.1 0.9 copy-start.13
  290.1 2.3 copy-start.6
  290.1 2.3 copy-start.8
  290.1 283.7 %all-gather.8.cloned.1.call-start = ((), (), s32[]{:S(2)}) async-start(), calls=%async_computation.8 | async-start | bytes 4866048 | tf_op jit(solution)/shard_map/all_gather | solution.py:127
  297.5 7.4 %copy-start.4 = (bf16[1024,4,32]{0,2,1:T(8,128)(2,1)S(1)}, bf16[1024,4,32]{0,2,1:T(8,128)(2,1)}, u32[]{:S(2)}) copy-start(bf16[1024,4,32]{0,2,1:T(8,128)(2,1)} %reshape.84) | copy-start | bytes 786436
  306.7 2.2 copy-start.9
  400.0 177.2 %copy-start.14 = (f32[128,256]{1,0:T(8,128)S(1)}, f32[128,256]{1,0:T(8,128)}, u32[]{:S(2)}) copy-start(f32[128,256]{1,0:T(8,128)} %get-tuple-element.51) | copy-start | bytes 393220
  (1 other events, 0.6 us)
Sparse Core Ops, SparseCore 0:
  9.8 60.3 all-gather.3
  72.7 76.6 reduce-scatter.4
  153.0 42.0 all-gather.5
  199.0 43.3 reduce-scatter.8
  244.8 41.9 reduce-scatter.10
  289.0 47.8 all-reduce.2
  339.6 58.2 reduce-scatter.6
  400.4 173.3 all-gather.7
